TPU v7x, 32 devices: a whole 2x2x4 slice. The times are simulated.
32 devices in a mesh: orb: 4 (over z), space: 8 (over y, x, core).
Axes of the slice: x: 2, y: 2, z: 4, core: 2. Of those that a mesh axis runs over, the one named last changes fastest.
Arguments:
- orbitals: float32 [32, 128, 128], P('orb', 'space'), may hold values from 0 to 0.25
- points: float32 [3, 128, 128], P(None, 'space')
- quad_weight: float32 [128, 128], P('space'), may hold values from 0.5 to 2
- external: float32 [128, 128], P('space'), may hold values from -3 to 1
- screening: float32 [32], replicated, may hold values from 0.05 to 2
- level_index: int32 [32], P('orb'), may hold values from 0 to 31
- near_cells: int32 [128, 27], P('space'), may hold values from -1 to 127, as said below
- far_cells: int32 [128, 42], P('space'), may hold values from -1 to 127, as said below
Outputs:
- new_orbitals: float32 [32, 128, 128], P('orb', 'space')
- hartree: float32 [128, 128], P('space')
Inputs may be any that keep to these rules, and one draw needn't show every extreme that they name: `near_cells`: row t lists distinct cells in increasing order, then -1: every cell of its own plane whose first two box indices differ from those of t by at most one (t itself among them), the cells directly above and below t, and some of the other cells of the two adjacent planes whose first two box indices differ from those of t by at most one. Some row holds 27 cells. `far_cells`: row t lists in increasing order, then -1, all cells of the planes floor(t / 16) - 1 to floor(t / 16) + 1 that are not in row t of near_cells. Some row holds 42 cells.
All inputs are finite; a program needn't handle non-finite values.
Results may differ from a plain program's by a relative error of at most 0.0003.
Values sent between devices are 32-bit elements; how exact they have to be, the bound alone decides.
No kernel may reach another device: no remote copies, remote signals or barrier semaphores. Data moves between devices by JAX's collectives and lax.ppermute only.
A program may use at most 64 MiB of HBM per device.

v0:
```python
import functools
import math

import jax
import jax.numpy as jnp
import numpy as np
from jax import lax
from jax.experimental import pallas as pl
from jax.experimental.pallas import tpu as pltpu
from jax.sharding import PartitionSpec as P

NODES = 4
LANES = 128
PLANE = 16
ROWS = 8
HALF = NODES**3

cell_side = 0.25
soften = 6.25e-06
green_scale = -0.5 / math.pi
log2e = math.log2(math.e)
highest = lax.Precision.HIGHEST

node_set = np.cos((2.0 * np.arange(NODES) + 1.0) * (math.pi / (2.0 * NODES)))
roots = [[node_set[m] for m in range(NODES) if m != a] for a in range(NODES)]
scales = [1.0 / np.prod([node_set[a] - r for r in roots[a]]) for a in range(NODES)]


def put_basis(cst):
    row = lax.broadcasted_iota(jnp.int32, (ROWS, LANES), 0)
    for i, pick in enumerate((row // 4, 2 + row // 4, row % 4)):
        for k in range(NODES):
            values = [float(scales[a] if k == NODES - 1 else roots[a][k]) for a in range(NODES)]
            made = jnp.full((ROWS, LANES), values[0], jnp.float32)
            for a in range(1, NODES):
                made = jnp.where(pick == a, values[a], made)
            cst[NODES * i + k] = made


def node_offsets():
    lane = lax.broadcasted_iota(jnp.int32, (1, LANES), 1) % HALF
    out = []
    for pick in (lane // 16, lane // 4 % 4, lane % 4):
        made = jnp.full((1, LANES), 0.5 * (node_set[0] + 1.0), jnp.float32)
        for a in range(1, NODES):
            made = jnp.where(pick == a, float(0.5 * (node_set[a] + 1.0)), made)
        out.append(made)
    return out


def poly(u, r0, r1, r2, scale):
    return ((u - r0) * (u - r1)) * ((u - r2) * scale)


def weights(cst, x, y, z, lows, sides):
    ux, uy, uz = (
        jnp.broadcast_to(2.0 * (c - lo) / e - 1.0, (ROWS, LANES)) for c, lo, e in zip((x, y, z), lows, sides)
    )
    pz = poly(uz, cst[8], cst[9], cst[10], cst[11])
    pyz = [poly(uy, cst[4 * k], cst[4 * k + 1], cst[4 * k + 2], cst[4 * k + 3]) * pz for k in range(2)]
    parts = []
    for a in range(NODES):
        px = poly(ux, *(float(r) for r in roots[a]), float(scales[a]))
        parts += [px * pyz[0], px * pyz[1]]
    return jnp.concatenate(parts, axis=0)


def twice(w):
    return jnp.concatenate([w, w], axis=0)


def cell_low(cell):
    return [(cell % 4).astype(jnp.float32) * cell_side, (cell // 4 % 4).astype(jnp.float32) * cell_side]


def dot_nt(a, b):
    return lax.dot_general(a, b, (((1,), (1,)), ((), ())), precision=highest, preferred_element_type=jnp.float32)


def gather_parts(block, axis, pairs, later=None):
    count = lax.axis_size(axis)
    parts = [block[None]]
    while sum(p.shape[0] for p in parts) < count:
        held = parts[0] if len(parts) == 1 else jnp.concatenate(parts, axis=0)
        have = held.shape[0]
        steps = range(1, 4 if (have > 1 or pairs) and have * 4 <= count else 2)
        parts = [held] + [lax.ppermute(held, axis, [(i, i ^ (have * j)) for i in range(count)]) for j in steps]
        if later is not None and have == 1:
            parts[1], later = lax.optimization_barrier((parts[1], later))
    return parts, later


def gather_list(block, axis):
    parts, _ = gather_parts(block, axis, True)
    return [p[k] for p in parts for k in range(p.shape[0])]


def lay_out(parts, whole):
    at = 0
    for part in parts:
        for k in range(part.shape[0]):
            whole[at + k] = part[k]
        at += part.shape[0]


def target_cell(me, t, groups):
    return t * groups + lax.bitwise_xor(jnp.int32(t) if isinstance(t, int) else t, me)


def split(v):
    high = v.astype(jnp.bfloat16)
    return high, (v - high.astype(jnp.float32)).astype(jnp.bfloat16)


def dot_bf16(a, b):
    return lax.dot_general(a, b, (((1,), (1,)), ((), ())), preferred_element_type=jnp.float32)


def dot_split(v, w):
    vh, vl = split(v)
    wh, wl = split(w)
    rows = v.shape[0]
    both = dot_bf16(jnp.concatenate([vh, vl], axis=0), wh)
    return both[:rows] + both[rows:] + dot_bf16(vh, wl)


def lane_sums(v):
    high, low = split(v)
    ones = jnp.ones((ROWS, 2 * v.shape[1]), jnp.bfloat16)
    return dot_bf16(ones, jnp.concatenate([high, low], axis=1))[0:1, :]


def charge_kernel(meta, own, partial, *refs):
    z_low = meta[0].astype(jnp.float32) * cell_side
    fields, (out, density, cst) = refs[:-3], refs[-3:]
    put_basis(cst)
    total = partial[...]
    for phi in fields:
        for j in range(phi.shape[0]):
            v = phi[j]
            total = total + v * v
    density[...] = 2.0 * total
    acc = jnp.zeros((HALF, LANES), jnp.float32)
    for c in range(PLANE):
        point = own[:, c, :]
        charge = point[4:5] * density[c : c + 1, :]
        low = (cell_side * (c % 4), cell_side * (c // 4), z_low)
        acc = acc + weights(cst, point[0:1], point[1:2], point[2:3], (0.0, 0.0, z_low), (1.0, 1.0, cell_side)) * charge
        moments = lane_sums(weights(cst, point[0:1], point[1:2], point[2:3], low, (cell_side,) * 3) * charge)
        out[c, :5, :] = point[:5]
        out[c, 5:6, :] = charge
        out[c, 6:7, :] = jnp.concatenate([moments, moments], axis=1)
    moments = lane_sums(acc)
    for c in range(PLANE):
        out[c, 7:8, :] = jnp.concatenate([moments, moments], axis=1)


def live_planes(me, planes):
    below = jnp.maximum(me - 1, 0)
    return below, below + jnp.maximum(planes - 2 - me, 0)


def list_lengths(lists, cell, slots, me, planes):
    low, high = jnp.int32(0), jnp.int32(slots[0])
    for _ in range(slots[0].bit_length()):
        mid = (low + high) // 2
        live = (low < high) & (lists[cell, jnp.minimum(mid, slots[0] - 1)] >= 0)
        high = jnp.where(live | (low >= high), high, mid)
        low = jnp.where(live, mid + 1, low)
    around = 1 + (me > 0).astype(jnp.int32) + (me + 1 < planes).astype(jnp.int32)
    return low, around * PLANE - low


def list_blocks(me, cell, lists, slots, planes, put_near, put_far, put_none, multiple):
    window = 3 * PLANE
    base = (me - 1) * PLANE
    below, n_planes = live_planes(me, planes)
    near_slots, far_slots = slots
    n_near, n_far = list_lengths(lists, cell, slots, me, planes)
    n_items = n_far + n_planes
    n_pairs = (n_items + 1) // 2

    def near_step(j, c):
        put_near(j, lists[cell, j] - base)
        return c

    lax.fori_loop(0, n_near, near_step, 0)

    def item(j):
        j = jnp.minimum(j, n_items - 1)
        p = j - n_far
        level = jnp.where(p < below, p, p + (me + 2 - below))
        slot = lists[cell, near_slots + jnp.minimum(j, far_slots - 1)] - base
        return jnp.where(j < n_far, slot, window + level)

    def far_step(j, c):
        put_far(n_near + j, item(2 * j), item(2 * j + 1), 2 * j + 1 < n_items)
        return c

    lax.fori_loop(0, n_pairs, far_step, 0)
    for u in range(multiple - 1):
        put_none(n_near + n_pairs + u)
    return n_near + n_pairs


def in_low_half():
    return lax.broadcasted_iota(jnp.int32, (1, LANES), 1) < HALF


def put_targets(pts, cell, tgt):
    for d in range(3):
        tgt[d] = jnp.broadcast_to(pts[PLANE + cell, d : d + 1, :], (LANES, LANES)).T


def each_square(tgt, src, first, count, use):
    sources = [[src[first + u, d : d + 1, :] for d in range(3)] for u in range(count)]
    for r in range(LANES // ROWS):
        at = [tgt[d, r * ROWS : (r + 1) * ROWS, :] for d in range(3)]
        for u in range(count):
            dx, dy, dz = (a - b for a, b in zip(at, sources[u]))
            use(r, u, (dx * dx + dy * dy) + (dz * dz + soften))


def cell_fields(message, c, groups, kinds):
    rows = kinds * PLANE
    return jnp.concatenate([message[pl.ds(g * rows + c, kinds, stride=PLANE), :] for g in range(groups)], axis=0)


def hartree_kernel(groups, kinds, unroll, slots, meta, lists, marks, mine, *refs):
    parts, (out, pts, src, every, items, tgt, sums, cst) = refs[:-8], refs[-8:]
    lay_out(parts, every)
    planes = every.shape[0]
    cells = PLANE // groups
    me, group = meta[0], meta[1]
    window = 3 * PLANE
    put_basis(cst)
    for k in range(3):
        there = lax.bitwise_xor(me, jnp.clip(me - 1 + k, 0, planes - 1))
        for c in range(PLANE):
            pts[k * PLANE + c] = every[there, c]
    row = lax.broadcasted_iota(jnp.int32, (ROWS, 1), 0)

    offsets = node_offsets()

    def item_of(lows, sides, moments):
        made = jnp.where(row == 5, moments, 0.0)
        for d in range(3):
            made = jnp.where(row == d, lows[d] + offsets[d] * sides[d], made)
        return made

    def put_cell(c, carry):
        lows = (*cell_low(c), (me - 1 + c // PLANE).astype(jnp.float32) * cell_side)
        items[c] = item_of(lows, (cell_side,) * 3, pts[c, 6:7, :])
        return carry

    lax.fori_loop(0, window, put_cell, 0, unroll=8)

    def put_plane(g, c):
        lows = (0.0, 0.0, g.astype(jnp.float32) * cell_side)
        items[window + g] = item_of(lows, (1.0, 1.0, cell_side), every[lax.bitwise_xor(me, g), 0, 7:8, :])
        return c

    lax.fori_loop(0, planes, put_plane, 0)
    items[window + planes] = jnp.zeros((ROWS, LANES), jnp.float32)
    low_half = in_low_half()
    z_low = me.astype(jnp.float32) * cell_side
    out[0] = jnp.broadcast_to(marks[...], (ROWS, LANES))

    def per_cell(t, carry):
        cell = target_cell(group, t, groups)

        def put_near(j, slot):
            src[t, j] = pts[slot]

        def put_far(j, first, second, live):
            src[t, j] = jnp.where(low_half, items[first], items[jnp.where(live, second, window + planes)])

        def put_none(j):
            src[t, j] = jnp.zeros((ROWS, LANES), jnp.float32)

        n_blocks = list_blocks(me, cell, lists, slots, planes, put_near, put_far, put_none, unroll)
        put_targets(pts, cell, tgt)

        def step(i, accs):
            accs = list(accs)
            charges = [src[t, unroll * i + u, 5:6, :] for u in range(unroll)]

            def use(r, u, sq):
                accs[r] = accs[r] + lax.rsqrt(sq) * charges[u]

            each_square(tgt, src.at[t], unroll * i, unroll, use)
            return tuple(accs)

        zero = jnp.zeros((ROWS, LANES), jnp.float32)
        accs = lax.fori_loop(0, (n_blocks + unroll - 1) // unroll, step, (zero,) * (LANES // ROWS))
        sums[t] = jnp.concatenate(accs, axis=0)
        return carry

    lax.fori_loop(0, cells, per_cell, 0)
    ones = jnp.ones((ROWS, LANES), jnp.float32)
    found = dot_nt(ones, sums[...].reshape(cells * LANES, LANES))
    total = jnp.zeros((groups * kinds, LANES), jnp.float32)
    for t in range(cells):
        cell = target_cell(group, t, groups)
        potential = found[0:1, t * LANES : (t + 1) * LANES]
        out[0, t : t + 1, :] = potential
        point = pts[PLANE + cell]
        scaled = point[4:5] * (point[3:4] + potential)
        v = cell_fields(mine, cell, groups, kinds) * scaled
        w = weights(cst, point[0:1], point[1:2], point[2:3], (0.0, 0.0, z_low), (1.0, 1.0, cell_side))
        total = total + dot_split(v, twice(w))
    for k in range(groups):
        out[1 + lax.bitwise_xor(group, k), :kinds, :] = total[k * kinds : (k + 1) * kinds, :]


def pairs_kernel(first, groups, planes, unroll, slots, meta, lists, pts, src, out, tgt):
    group = meta[1]
    _, n_planes = live_planes(meta[0], planes)

    def per_cell(t, carry):
        cell = target_cell(group, first + t, groups)
        put_targets(pts, cell, tgt)
        n_near, n_far = list_lengths(lists, cell, slots, meta[0], planes)
        n_blocks = n_near + (n_far + n_planes + 1) // 2

        def measure(i, x):
            def use(r, u, sq):
                out[t, unroll * i + u, r * ROWS : (r + 1) * ROWS, :] = sq

            each_square(tgt, src.at[first + t], unroll * i, unroll, use)
            return x

        lax.fori_loop(0, (n_blocks + unroll - 1) // unroll, measure, 0)
        return carry

    lax.fori_loop(0, out.shape[0], per_cell, 0)


def combine_kernel(kinds, meta, *refs):
    shares, (hartree, out, total) = refs[:-3], refs[-3:]
    groups = len(shares)
    for k, share in enumerate(shares):
        for t in range(PLANE // groups):
            cell = target_cell(lax.bitwise_xor(meta[1], k), t, groups)
            out[pl.ds(cell, 1), :] = share[0, t : t + 1, :]
    hartree[...] = out[:PLANE, :]
    for g in range(groups):
        added = shares[0][1 + g, :kinds, :]
        for share in shares[1:]:
            added = added + share[1 + g, :kinds, :]
        total[g * kinds : (g + 1) * kinds, :] = added
    rows = groups * kinds // 2
    low_half = lax.broadcasted_iota(jnp.int32, (1, LANES), 1) < HALF
    out[PLANE:, :] = jnp.where(low_half, total[:rows, :], total[rows:, :])


def orbital_kernel(
    planes, batch, unit, steps, slots, n_squares, meta, lists, levels, rates_of,
    pts, before, mine, after, *refs,
):
    squares, refs = refs[:n_squares], refs[n_squares:]
    parts, (out, rate, slot_of, units, every, val, mom, srcv, dist, inv, acc, cst) = refs[:-12], refs[-12:]
    lay_out(parts, every)
    groups, cells, kinds, _ = out.shape
    orbs = groups * kinds
    n_rates = rates_of.shape[0]
    me, group = meta[0], meta[1]

    def clear(i, c):
        slot_of[i] = -1
        rate[i] = 0.0
        return c

    lax.fori_loop(0, n_rates, clear, 0)
    for q in range(2 * batch):
        rate[n_rates + q] = 0.0
    lane = lax.broadcasted_iota(jnp.int32, (1, LANES), 1) % orbs

    def rank(i, carry):
        found, lane_slot = carry
        level = levels[i]
        known = slot_of[level]
        slot = jnp.where(known < 0, found, known)
        slot_of[level] = slot
        rate[slot] = rates_of[level]
        return found + (known < 0).astype(jnp.int32), jnp.where(lane == i, slot, lane_slot)

    n_levels, lane_slot = lax.fori_loop(0, orbs, rank, (jnp.int32(0), jnp.zeros((1, LANES), jnp.int32)))
    n_batches = (n_levels + batch - 1) // batch
    first_half = lax.broadcasted_iota(jnp.int32, (1, 2 * orbs), 1) < orbs
    put_basis(cst)

    def flip(v):
        high = v.astype(jnp.bfloat16).astype(jnp.float32)
        square = jnp.concatenate([high, v - high, jnp.zeros((LANES - 2 * orbs, LANES), jnp.float32)], axis=0)
        return square.T[:, : 2 * orbs].astype(jnp.bfloat16)

    for k in range(3):
        message = (before, mine, after)[k]
        there = lax.bitwise_xor(me, jnp.clip(me - 1 + k, 0, planes - 1))

        def prepare(c, carry):
            at = k * PLANE + c
            point = pts[at]
            potential = point[3:4] + every[there, pl.ds(c, 1), :]
            v = cell_fields(message, c, groups, kinds) * (point[4:5] * potential)
            val[at] = flip(v)
            vh, vl = split(v)
            z_low = (me - 1 + k).astype(jnp.float32) * cell_side
            low = (*cell_low(c), z_low)
            wh, wl = split(weights(cst, point[0:1], point[1:2], point[2:3], low, (cell_side,) * 3))
            all_of = dot_bf16(jnp.concatenate([wh, wl], axis=0), jnp.concatenate([vh, vh, vl, vl], axis=0))
            m = all_of[:HALF] + all_of[HALF:]
            m = m[:, : 2 * orbs] + pltpu.roll(all_of[:HALF], 2 * orbs, 1)[:, : 2 * orbs]
            high = m.astype(jnp.bfloat16).astype(jnp.float32)
            mom[at] = jnp.where(first_half, high, m - high).astype(jnp.bfloat16)
            return carry

        lax.fori_loop(0, PLANE, prepare, 0, unroll=4)

    def put_plane(g, c):
        there = lax.bitwise_xor(me, g)
        rows = []
        for k in range(groups):
            row = lax.bitwise_xor(group, k) * kinds
            v = every[there, pl.ds(PLANE + lax.rem(row, orbs // 2), kinds), :]
            rows.append(jnp.where(row < orbs // 2, v, pltpu.roll(v, HALF, 1)))
        mom[3 * PLANE + g] = flip(jnp.concatenate(rows, axis=0))[:HALF]
        return c

    lax.fori_loop(0, planes, put_plane, 0)

    def products(g, b, first):
        rates = [rate[b * batch + q] for q in range(batch)]
        rows = []
        for q in range(batch):
            tiles = [
                (jnp.exp2(dist[g, first + h] * rates[q]) * inv[g, first + h]).astype(jnp.bfloat16) for h in range(unit)
            ]
            rows.append(jnp.concatenate(tiles, axis=1))
        v = jnp.concatenate([srcv[g, first + h] for h in range(unit)], axis=0)
        return jnp.dot(jnp.concatenate(rows, axis=0), v, preferred_element_type=jnp.float32)

    share = cells // n_squares

    def per_group(p, carry):
        def list_cell(g, x):
            def put_near(j, slot):
                srcv[g, j] = val[slot]

            def put_far(j, first, second, live):
                srcv[g, j, :HALF, :] = mom[first]
                srcv[g, j, HALF:, :] = jnp.where(live, mom[second], jnp.zeros_like(mom[second]))

            def put_none(j):
                srcv[g, j] = jnp.zeros(srcv.shape[2:], srcv.dtype)

            cell = target_cell(group, p * share + g, groups)
            n_blocks = list_blocks(me, cell, lists, slots, planes, put_near, put_far, put_none, unit)
            units[g] = (n_blocks + unit - 1) // unit

            def clear_acc(b, y):
                acc[g, b] = jnp.zeros(acc.shape[2:], jnp.float32)
                return y

            lax.fori_loop(0, n_batches, clear_acc, 0)
            return x

        lax.fori_loop(0, share, list_cell, 0)

        for k in range(n_squares):

            @pl.when(p == k)
            def _():
                for g in range(share):

                    def measure(i, x):
                        for u in range(unit):
                            sq = squares[k][g, unit * i + u]
                            one_over = lax.rsqrt(sq)
                            inv[g, unit * i + u] = one_over
                            dist[g, unit * i + u] = sq * one_over
                        return x

                    lax.fori_loop(0, units[g], measure, 0)

        def step(i, at):
            g, b, u = at
            for _ in range(steps):
                acc[g, b] = acc[g, b] + products(g, b, unit * u)
                wrap = u + 1 >= units[g]
                later = jnp.where(wrap, b + 1, b)
                over, last = later >= n_batches, g + 1 >= share
                u = jnp.where(wrap, 0, u + 1)
                b = jnp.where(over, jnp.where(last, n_batches, 0), later)
                g = jnp.where(over & jnp.logical_not(last), g + 1, g)
            return g, b, u

        work = sum(units[g] for g in range(share)) * n_batches
        zero = jnp.int32(0)
        lax.fori_loop(0, (work + steps - 1) // steps, step, (zero, zero, zero))

        def finish(g, x):
            def choose(b, add):
                for q in range(batch):
                    mine = lane_slot[:, : 2 * orbs] == b * batch + q
                    add = add + jnp.where(mine, acc[g, b, q * LANES : (q + 1) * LANES, :], 0.0)
                return add

            total = lax.fori_loop(0, n_batches, choose, jnp.zeros((LANES, 2 * orbs), jnp.float32))
            flipped = jnp.concatenate([total, jnp.zeros((LANES, LANES - 2 * orbs), jnp.float32)], axis=1).T
            rows = (flipped[:orbs] + flipped[orbs : 2 * orbs]) * green_scale
            for k in range(groups):
                out[k, p * share + g] = rows[k * kinds : (k + 1) * kinds]
            return x

        lax.fori_loop(0, share, finish, 0)
        return carry

    lax.fori_loop(0, n_squares, per_group, 0)


def place_kernel(meta, *refs):
    parts, out, ordered = refs[:-2], refs[-2], refs[-1]
    for k, part in enumerate(parts):
        for t in range(part.shape[0]):
            ordered[target_cell(lax.bitwise_xor(meta[1], k), t, len(parts))] = part[t]
    for c in range(PLANE):
        out[:, c, :] = ordered[c]


def smem():
    return pl.BlockSpec(memory_space=pltpu.SMEM)


def vmem():
    return pl.BlockSpec(memory_space=pltpu.VMEM)


def call(kernel, name, out_shape, smems, args, scratch=(), mib=8):
    return pl.pallas_call(
        kernel,
        out_shape=out_shape,
        in_specs=[smem()] * smems + [vmem()] * (len(args) - smems),
        out_specs=jax.tree.map(lambda _: vmem(), out_shape),
        scratch_shapes=scratch,
        compiler_params=pltpu.CompilerParams(vmem_limit_bytes=mib * 1024 * 1024),
        name=name,
    )(*args)


def body(orbitals, points, quad_weight, external, screening, level_index, near_cells, far_cells):
    kinds, cells, point_count = orbitals.shape
    planes, groups = lax.axis_size("space"), lax.axis_size("orb")
    orbs = kinds * groups
    window = 3 * PLANE
    share = cells // groups
    me, group = lax.axis_index("space"), lax.axis_index("orb")
    meta = jnp.stack([me, group]).astype(jnp.int32)
    f32, bf16 = jnp.float32, jnp.bfloat16

    fields = gather_list(orbitals, "orb")
    weight = quad_weight * (cell_side**3 / point_count)
    own = jnp.concatenate([points, external[None], weight[None], jnp.zeros((3, cells, LANES), f32)], axis=0)
    marks = jnp.pad(level_index.astype(f32), (0, LANES - kinds))[None]
    ends = planes - 1
    up = [(i, i + 1) for i in range(ends)]
    down = [(i + 1, i) for i in range(ends)]
    slots = (near_cells.shape[1], far_cells.shape[1])
    lists = jnp.concatenate([near_cells, far_cells], axis=1)
    partial = jnp.sum(orbitals * orbitals, axis=0)
    basis = pltpu.VMEM((3 * NODES, ROWS, LANES), f32)

    charges = call(
        charge_kernel,
        "charge",
        jax.ShapeDtypeStruct((cells, ROWS, LANES), f32),
        1,
        (meta, own, partial, *fields[1:]),
        [pltpu.VMEM((cells, LANES), f32), basis],
    )
    mine = jnp.concatenate([f.reshape(kinds * cells, LANES) for f in fields], axis=0)
    charges, mine = gather_parts(charges, "space", False, mine)
    before = lax.ppermute(mine, "space", up)

    batch, unit, steps = 4, 4, 18
    most = near_cells.shape[1]
    blocks = most + (window - most + planes - 2) // 2 + unit - 1
    blocks = -(-blocks // unit) * unit
    shares, pts, src = call(
        functools.partial(hartree_kernel, groups, kinds, unit, slots),
        "hartree",
        (
            jax.ShapeDtypeStruct((1 + groups, ROWS, LANES), f32),
            jax.ShapeDtypeStruct((window, ROWS, LANES), f32),
            jax.ShapeDtypeStruct((share, blocks, ROWS, LANES), f32),
        ),
        2,
        (meta, lists, marks, mine, *charges),
        [
            pltpu.VMEM((planes, cells, ROWS, LANES), f32),
            pltpu.VMEM((window + planes + 1, ROWS, LANES), f32),
            pltpu.VMEM((3, LANES, LANES), f32),
            pltpu.VMEM((share, LANES, LANES), f32),
            basis,
        ],
        12,
    )
    mine, shares = lax.optimization_barrier((mine, shares))
    after = lax.ppermute(mine, "space", down)
    n_squares = 2 if share % 2 == 0 else 1

    def distances(k, src):
        return call(
            functools.partial(pairs_kernel, k * share // n_squares, groups, planes, unit, slots),
            "pairs",
            jax.ShapeDtypeStruct((share // n_squares, blocks, LANES, LANES), f32),
            2,
            (meta, lists, pts, src),
            [pltpu.VMEM((3, LANES, LANES), f32)],
            4,
        )

    squares = [distances(0, src)]
    shares = gather_list(shares, "orb")
    levels = jnp.concatenate([share[0, ROWS - 1, :kinds] for share in shares]).astype(jnp.int32)
    hartree, combined = call(
        functools.partial(combine_kernel, kinds),
        "combine",
        (jax.ShapeDtypeStruct((cells, LANES), f32), jax.ShapeDtypeStruct((cells + orbs // 2, LANES), f32)),
        1,
        (meta, *shares),
        [pltpu.VMEM((orbs, LANES), f32)],
    )
    gathered, src = gather_parts(combined, "space", False, src)
    if n_squares > 1:
        squares.append(distances(1, src))

    levels_at_most = -(-screening.shape[0] // batch) + 1
    sent = call(
        functools.partial(orbital_kernel, planes, batch, unit, steps, slots, n_squares),
        "orbitals",
        jax.ShapeDtypeStruct((groups, share, kinds, LANES), f32),
        4,
        (meta, lists, levels, screening * (-log2e), pts, before, mine, after, *squares, *gathered),
        [
            pltpu.SMEM((screening.shape[0] + 2 * batch,), f32),
            pltpu.SMEM((screening.shape[0],), jnp.int32),
            pltpu.SMEM((share,), jnp.int32),
            pltpu.VMEM((planes, cells + orbs // 2, LANES), f32),
            pltpu.VMEM((window, LANES, 2 * orbs), bf16),
            pltpu.VMEM((window + planes, HALF, 2 * orbs), bf16),
            pltpu.VMEM((share // n_squares, blocks, LANES, 2 * orbs), bf16),
            pltpu.VMEM((share // n_squares, blocks, LANES, LANES), f32),
            pltpu.VMEM((share // n_squares, blocks, LANES, LANES), f32),
            pltpu.VMEM((share // n_squares, levels_at_most, batch * LANES, 2 * orbs), f32),
            basis,
        ],
        28,
    )
    parts = [sent[0]]
    for k in range(1, groups):
        parts.append(lax.ppermute(sent[k], "orb", [(i, i ^ k) for i in range(groups)]))
    updated = call(
        place_kernel,
        "place",
        jax.ShapeDtypeStruct((kinds, cells, LANES), f32),
        1,
        (meta, *parts),
        [pltpu.VMEM((cells, kinds, LANES), f32)],
    )
    return updated, hartree


def solution(mesh):
    in_specs = (
        P("orb", "space", None),
        P(None, "space", None),
        P("space", None),
        P("space", None),
        P(),
        P("orb"),
        P("space", None),
        P("space", None),
    )
    out_specs = (P("orb", "space", None), P("space", None))
    return jax.shard_map(body, mesh=mesh, in_specs=in_specs, out_specs=out_specs, check_vma=False)
```

profile of v0, /device:TPU:4, one launch (start us, length us, event | category | flops | bytes accessed | tf_op | source)
XLA Modules:
  0.0 99.3 jit_solution(13991886573705530629)
XLA Ops:
  0.6 1.6 %collective-permute-start = (f32[1,8,16,128]{3,2,1,0:T(8,128)}, f32[1,8,16,128]{3,2,1,0:T(8,128)S(1)}, u32[]{:S(2)}, u32[]{:S(2)}) collective-permute-start(f32[1,8,16,128]{3,2,1,0:T(8,128)} %bitcast.56), channel_id=1, source_target_pairs={{0,8},{8,0},{16,24},{24,16},{1,9},{9,1},{17,25},{25,17},{2,10},{10... | collective-permute-start | bytes 196616 | tf_op jit(solution)/shard_map/ppermute | solution.py:87
  2.3 2.6 %collective-permute-start.1 = (f32[1,8,16,128]{3,2,1,0:T(8,128)}, f32[1,8,16,128]{3,2,1,0:T(8,128)S(1)}, u32[]{:S(2)}, u32[]{:S(2)}) collective-permute-start(f32[1,8,16,128]{3,2,1,0:T(8,128)} %bitcast.57), channel_id=1, source_target_pairs={{0,16},{8,24},{16,0},{24,8},{1,17},{9,25},{17,1},{25,9},{2,18},{10... | collective-permute-start | bytes 196616 | tf_op jit(solution)/shard_map/ppermute | solution.py:87
  4.9 0.2 collective-permute-start.2
  5.1 0.7 multiply_bitcast_fusion
  5.8 0.7 convert_element_type.8
  6.4 0.7 broadcast_multiply_fusion.rates_of
  7.1 0.1 pad.20.clone
  7.2 1.0 maximum_maximum_fusion
  8.1 0.1 pad_add_fusion.1.meta
  8.2 0.0 collective-permute-done
  8.2 1.6 %collective-permute-done.1 = f32[1,8,16,128]{3,2,1,0:T(8,128)S(1)} collective-permute-done((f32[1,8,16,128]{3,2,1,0:T(8,128)}, f32[1,8,16,128]{3,2,1,0:T(8,128)S(1)}, u32[]{:S(2)}, u32[]{:S(2)}) %collective-permute-start.1) | collective-permute-done | bytes 65568 | tf_op jit(solution)/shard_map/ppermute | solution.py:87
  9.8 1.4 %collective-permute-done.2 = f32[1,8,16,128]{3,2,1,0:T(8,128)S(1)} collective-permute-done((f32[1,8,16,128]{3,2,1,0:T(8,128)}, f32[1,8,16,128]{3,2,1,0:T(8,128)S(1)}, u32[]{:S(2)}, u32[]{:S(2)}) %collective-permute-start.2) | collective-permute-done | bytes 65568 | tf_op jit(solution)/shard_map/ppermute | solution.py:87
  11.2 1.1 %charge.1 = f32[16,8,128]{2,1,0:T(8,128)S(1)} custom-call(s32[2]{0:T(128)S(1)} %pad_add_fusion.1.meta, f32[8,16,128]{2,1,0:T(8,128)S(1)} %get-tuple-element.28.own, f32[16,128]{1,0:T(8,128)S(1)} %get-tuple-element.29.partial, f32[8,16,128]{2,1,0:T(8,128)S(1)} %bitcast.39, f32[8,16,128]{2,1,0:T(8,128)S(1)} %bitcast.41, f32[8,16,128]{2,1,0:T(8,128)S(1)} %bitcast.43), custom_call_target="tpu_custom_call" | custom-call | tf_op jit(solution)/shard_map/charge/pallas_call | solution.py:541
  12.3 0.0 collective-permute-start.3
  12.3 0.9 pad_maximum_fusion.mine
  13.1 0.4 collective-permute-done.3
  13.5 1.6 %collective-permute-start.4 = (f32[2,16,8,128]{3,2,1,0:T(8,128)S(1)}, f32[2,16,8,128]{3,2,1,0:T(8,128)S(1)}, u32[]{:S(2)}, u32[]{:S(2)}) collective-permute-start(f32[2,16,8,128]{3,2,1,0:T(8,128)S(1)} %pad_maximum_fusion.1.refs_0_), channel_id=1, source_target_pairs={{0,2},{1,3},{2,0},{3,1},{4,6},{5,7},{6,4},{7,5},{8,10},{9,11},{10,... | collective-permute-start | bytes 393224 | tf_op jit(solution)/shard_map/ppermute | solution.py:87
  15.1 0.5 collective-permute-start.5
  15.6 1.5 %collective-permute-start.6 = (f32[2,16,8,128]{3,2,1,0:T(8,128)S(1)}, f32[2,16,8,128]{3,2,1,0:T(8,128)S(1)}, u32[]{:S(2)}, u32[]{:S(2)}) collective-permute-start(f32[2,16,8,128]{3,2,1,0:T(8,128)S(1)} %pad_maximum_fusion.1.refs_0_), channel_id=1, source_target_pairs={{0,6},{1,7},{2,4},{3,5},{4,2},{5,3},{6,0},{7,1},{8,14},{9,15},{10,... | collective-permute-start | bytes 393224 | tf_op jit(solution)/shard_map/ppermute | solution.py:87
  17.1 0.8 pad_add_fusion.lists
  17.9 1.9 %collective-permute-start.10 = (f32[512,128]{1,0:T(8,128)S(1)}, f32[512,128]{1,0:T(8,128)S(1)}, u32[]{:S(2)}, u32[]{:S(2)}) collective-permute-start(f32[512,128]{1,0:T(8,128)S(1)} %pad_maximum_fusion.mine), channel_id=1, source_target_pairs={{0,1},{1,2},{2,3},{3,4},{4,5},{5,6},{6,7},{8,9},{9,10},{10,11},{11... | collective-permute-start | bytes 786440 | tf_op jit(solution)/shard_map/ppermute | solution.py:584
  19.8 0.0 collective-permute-done.4.refs_1_
  19.8 3.4 %collective-permute-done.5.refs_2_ = f32[2,16,8,128]{3,2,1,0:T(8,128)S(1)} collective-permute-done((f32[2,16,8,128]{3,2,1,0:T(8,128)S(1)}, f32[2,16,8,128]{3,2,1,0:T(8,128)S(1)}, u32[]{:S(2)}, u32[]{:S(2)}) %collective-permute-start.5) | collective-permute-done | bytes 131104 | tf_op jit(solution)/shard_map/ppermute | solution.py:87
  23.2 0.0 collective-permute-done.6.refs_3_
  23.2 8.9 %hartree.1 = (f32[5,8,128]{2,1,0:T(8,128)S(1)}, f32[48,8,128]{2,1,0:T(8,128)S(1)}, f32[4,44,8,128]{3,2,1,0:T(8,128)S(1)}) custom-call(s32[2]{0:T(128)S(1)} %pad_add_fusion.1.meta, s32[16,69]{1,0:T(8,128)S(1)} %pad_add_fusion.lists, f32[1,128]{1,0:T(1,128)S(1)} %pad_bitcast_fusion.marks, f32[512,128]{1,0:T(8,128)S(1)} %pad_maximum_fusion.mine, ...), custom_call_target="tpu_custom_call" | custom-call | tf_op jit(solution)/shard_map/hartree/pallas_call | solution.py:541
  32.1 0.0 collective-permute-start.7
  32.1 2.3 %collective-permute-start.8 = (f32[1,5,8,128]{3,2,1,0:T(8,128)S(1)}, f32[1,5,8,128]{3,2,1,0:T(8,128)S(1)}, u32[]{:S(2)}, u32[]{:S(2)}) collective-permute-start(f32[1,5,8,128]{3,2,1,0:T(8,128)S(1)} %bitcast.46), channel_id=1, source_target_pairs={{0,16},{8,24},{16,0},{24,8},{1,17},{9,25},{17,1},{25,9},{2,18},{10... | collective-permute-start | bytes 61448 | tf_op jit(solution)/shard_map/ppermute | solution.py:87
  34.5 2.1 %collective-permute-start.9 = (f32[1,5,8,128]{3,2,1,0:T(8,128)S(1)}, f32[1,5,8,128]{3,2,1,0:T(8,128)S(1)}, u32[]{:S(2)}, u32[]{:S(2)}) collective-permute-start(f32[1,5,8,128]{3,2,1,0:T(8,128)S(1)} %bitcast.47), channel_id=1, source_target_pairs={{0,24},{8,16},{16,8},{24,0},{1,25},{9,17},{17,9},{25,1},{2,26},{10... | collective-permute-start | bytes 61448 | tf_op jit(solution)/shard_map/ppermute | solution.py:87
  36.5 1.9 %collective-permute-start.11 = (f32[512,128]{1,0:T(8,128)S(1)}, f32[512,128]{1,0:T(8,128)S(1)}, u32[]{:S(2)}, u32[]{:S(2)}) collective-permute-start(f32[512,128]{1,0:T(8,128)S(1)} %pad_maximum_fusion.mine), channel_id=1, source_target_pairs={{1,0},{2,1},{3,2},{4,3},{5,4},{6,5},{7,6},{9,8},{10,9},{11,10},{12... | collective-permute-start | bytes 786440 | tf_op jit(solution)/shard_map/ppermute | solution.py:610
  38.5 2.3 %pairs.2.refs_0_ = f32[2,44,128,128]{3,2,1,0:T(8,128)S(1)} custom-call(s32[2]{0:T(128)S(1)} %pad_add_fusion.1.meta, s32[16,69]{1,0:T(8,128)S(1)} %pad_add_fusion.lists, f32[48,8,128]{2,1,0:T(8,128)S(1)} %get-tuple-element.17.pts, f32[4,44,8,128]{3,2,1,0:T(8,128)S(1)} %get-tuple-element.21.src), custom_call_target="tpu_custom_call" | custom-call | tf_op jit(solution)/shard_map/pairs/pallas_call | solution.py:541
  40.8 0.0 collective-permute-done.9
  40.8 0.0 collective-permute-done.8
  40.8 0.0 collective-permute-done.7
  40.9 1.2 %combine.1 = (f32[16,128]{1,0:T(8,128)}, f32[32,128]{1,0:T(8,128)S(1)}) custom-call(s32[2]{0:T(128)S(1)} %pad_add_fusion.1.meta, f32[5,8,128]{2,1,0:T(8,128)S(1)} %get-tuple-element.16.refs_0_, f32[5,8,128]{2,1,0:T(8,128)S(1)} %bitcast.48, f32[5,8,128]{2,1,0:T(8,128)S(1)} %bitcast.51, f32[5,8,128]{2,1,0:T(8,128)S(1)} %bitcast.53), custom_call_target="tpu_custom_call" | custom-call | tf_op jit(solution)/shard_map/combine/pallas_call | solution.py:541
  42.0 0.6 collective-permute-start.12
  42.6 0.8 collective-permute-done.12
  43.4 0.2 collective-permute-start.13
  43.6 1.5 %collective-permute-start.14 = (f32[2,32,128]{2,1,0:T(8,128)S(1)}, f32[2,32,128]{2,1,0:T(8,128)S(1)}, u32[]{:S(2)}, u32[]{:S(2)}) collective-permute-start(f32[2,32,128]{2,1,0:T(8,128)S(1)} %pad_maximum_fusion.2.refs_2_), channel_id=1, source_target_pairs={{0,4},{1,5},{2,6},{3,7},{4,0},{5,1},{6,2},{7,3},{8,12},{9,13},{10,... | collective-permute-start | bytes 98312 | tf_op jit(solution)/shard_map/ppermute | solution.py:87
  45.1 1.8 %collective-permute-start.15 = (f32[2,32,128]{2,1,0:T(8,128)S(1)}, f32[2,32,128]{2,1,0:T(8,128)S(1)}, u32[]{:S(2)}, u32[]{:S(2)}) collective-permute-start(f32[2,32,128]{2,1,0:T(8,128)S(1)} %pad_maximum_fusion.2.refs_2_), channel_id=1, source_target_pairs={{0,6},{1,7},{2,4},{3,5},{4,2},{5,3},{6,0},{7,1},{8,14},{9,15},{10,... | collective-permute-start | bytes 98312 | tf_op jit(solution)/shard_map/ppermute | solution.py:87
  46.9 0.1 maximum_convert_fusion.levels
  47.0 2.4 %pairs.3.refs_1_ = f32[2,44,128,128]{3,2,1,0:T(8,128)S(1)} custom-call(s32[2]{0:T(128)S(1)} %pad_add_fusion.1.meta, s32[16,69]{1,0:T(8,128)S(1)} %pad_add_fusion.lists, f32[48,8,128]{2,1,0:T(8,128)S(1)} %get-tuple-element.17.pts, f32[4,44,8,128]{3,2,1,0:T(8,128)S(1)} %get-tuple-element.21.src), custom_call_target="tpu_custom_call" | custom-call | tf_op jit(solution)/shard_map/pairs/pallas_call | solution.py:541
  49.4 0.0 collective-permute-done.13.refs_3_
  49.4 0.0 collective-permute-done.14.refs_4_
  49.5 0.5 collective-permute-done.15.refs_5_
  49.9 0.0 collective-permute-done.10.before
  49.9 0.0 collective-permute-done.11.after
  49.9 40.4 %orbitals.1 = f32[4,4,8,128]{3,2,1,0:T(8,128)S(1)} custom-call(s32[2]{0:T(128)S(1)} %pad_add_fusion.1.meta, s32[16,69]{1,0:T(8,128)S(1)} %pad_add_fusion.lists, s32[32]{0:T(128)S(1)} %maximum_convert_fusion.levels, f32[32]{0:T(128)S(1)} %broadcast_multiply_fusion.rates_of, f32[48,8,128]{2,1,0:T(8,128)S(1)} %get-tuple-element.17.pts, ...), custom_call_target="tpu_custom_call" | custom-call | tf_op jit(solution)/shard_map/orbitals/pallas_call | solution.py:541
  90.4 0.1 collective-permute-start.16
  90.4 2.1 %collective-permute-start.17 = (f32[4,8,128]{2,1,0:T(8,128)S(1)}, f32[4,8,128]{2,1,0:T(8,128)S(1)}, u32[]{:S(2)}, u32[]{:S(2)}) collective-permute-start(f32[4,8,128]{2,1,0:T(8,128)S(1)} %get-tuple-element.25), channel_id=1, source_target_pairs={{0,16},{8,24},{16,0},{24,8},{1,17},{9,25},{17,1},{25,9},{2,18},{10... | collective-permute-start | bytes 49160 | tf_op jit(solution)/shard_map/ppermute | solution.py:663
  92.6 2.2 %collective-permute-start.18 = (f32[4,8,128]{2,1,0:T(8,128)S(1)}, f32[4,8,128]{2,1,0:T(8,128)S(1)}, u32[]{:S(2)}, u32[]{:S(2)}) collective-permute-start(f32[4,8,128]{2,1,0:T(8,128)S(1)} %get-tuple-element.24), channel_id=1, source_target_pairs={{0,24},{8,16},{16,8},{24,0},{1,25},{9,17},{17,9},{25,1},{2,26},{10... | collective-permute-start | bytes 49160 | tf_op jit(solution)/shard_map/ppermute | solution.py:663
  94.8 0.0 collective-permute-done.16.refs_1_
  94.8 0.3 collective-permute-done.17.refs_2_
  95.1 3.0 %collective-permute-done.18.refs_3_ = f32[4,8,128]{2,1,0:T(8,128)S(1)} collective-permute-done((f32[4,8,128]{2,1,0:T(8,128)S(1)}, f32[4,8,128]{2,1,0:T(8,128)S(1)}, u32[]{:S(2)}, u32[]{:S(2)}) %collective-permute-start.18) | collective-permute-done | bytes 16416 | tf_op jit(solution)/shard_map/ppermute | solution.py:663
  98.1 1.2 %place.1 = f32[8,16,128]{2,1,0:T(8,128)} custom-call(s32[2]{0:T(128)S(1)} %pad_add_fusion.1.meta, f32[4,8,128]{2,1,0:T(8,128)S(1)} %get-tuple-element.27.refs_0_, f32[4,8,128]{2,1,0:T(8,128)S(1)} %collective-permute-done.16.refs_1_, f32[4,8,128]{2,1,0:T(8,128)S(1)} %collective-permute-done.17.refs_2_, f32[4,8,128]{2,1,0:T(8,128)S(1)} %collective-permute-done.18.refs_3_), custom_call_target="tpu_custom_call" | custom-call | tf_op jit(solution)/shard_map/place/pallas_call | solution.py:541
  (9 shorter events, 0.0 us)
Async XLA Ops:
  0.6 7.6 %collective-permute-start = (f32[1,8,16,128]{3,2,1,0:T(8,128)}, f32[1,8,16,128]{3,2,1,0:T(8,128)S(1)}, u32[]{:S(2)}, u32[]{:S(2)}) collective-permute-start(f32[1,8,16,128]{3,2,1,0:T(8,128)} %bitcast.56), channel_id=1, source_target_pairs={{0,8},{8,0},{16,24},{24,16},{1,9},{9,1},{17,25},{25,17},{2,10},{10... | collective-permute-start | bytes 196616 | tf_op jit(solution)/shard_map/ppermute | solution.py:87
  2.3 7.5 %collective-permute-start.1 = (f32[1,8,16,128]{3,2,1,0:T(8,128)}, f32[1,8,16,128]{3,2,1,0:T(8,128)S(1)}, u32[]{:S(2)}, u32[]{:S(2)}) collective-permute-start(f32[1,8,16,128]{3,2,1,0:T(8,128)} %bitcast.57), channel_id=1, source_target_pairs={{0,16},{8,24},{16,0},{24,8},{1,17},{9,25},{17,1},{25,9},{2,18},{10... | collective-permute-start | bytes 196616 | tf_op jit(solution)/shard_map/ppermute | solution.py:87
  4.9 6.3 %collective-permute-start.2 = (f32[1,8,16,128]{3,2,1,0:T(8,128)}, f32[1,8,16,128]{3,2,1,0:T(8,128)S(1)}, u32[]{:S(2)}, u32[]{:S(2)}) collective-permute-start(f32[1,8,16,128]{3,2,1,0:T(8,128)} %bitcast.58), channel_id=1, source_target_pairs={{0,24},{8,16},{16,8},{24,0},{1,25},{9,17},{17,9},{25,1},{2,26},{10... | collective-permute-start | bytes 196616 | tf_op jit(solution)/shard_map/ppermute | solution.py:87
  12.3 1.3 %collective-permute-start.3 = (f32[1,16,8,128]{3,2,1,0:T(8,128)S(1)}, f32[1,16,8,128]{3,2,1,0:T(8,128)S(1)}, u32[]{:S(2)}, u32[]{:S(2)}) collective-permute-start(f32[1,16,8,128]{3,2,1,0:T(8,128)S(1)} %bitcast.37), channel_id=1, source_target_pairs={{0,1},{1,0},{2,3},{3,2},{4,5},{5,4},{6,7},{7,6},{8,9},{9,8},{10,11... | collective-permute-start | bytes 196616 | tf_op jit(solution)/shard_map/ppermute | solution.py:87
  13.5 6.3 %collective-permute-start.4 = (f32[2,16,8,128]{3,2,1,0:T(8,128)S(1)}, f32[2,16,8,128]{3,2,1,0:T(8,128)S(1)}, u32[]{:S(2)}, u32[]{:S(2)}) collective-permute-start(f32[2,16,8,128]{3,2,1,0:T(8,128)S(1)} %pad_maximum_fusion.1.refs_0_), channel_id=1, source_target_pairs={{0,2},{1,3},{2,0},{3,1},{4,6},{5,7},{6,4},{7,5},{8,10},{9,11},{10,... | collective-permute-start | bytes 393224 | tf_op jit(solution)/shard_map/ppermute | solution.py:87
  15.1 8.1 %collective-permute-start.5 = (f32[2,16,8,128]{3,2,1,0:T(8,128)S(1)}, f32[2,16,8,128]{3,2,1,0:T(8,128)S(1)}, u32[]{:S(2)}, u32[]{:S(2)}) collective-permute-start(f32[2,16,8,128]{3,2,1,0:T(8,128)S(1)} %pad_maximum_fusion.1.refs_0_), channel_id=1, source_target_pairs={{0,4},{1,5},{2,6},{3,7},{4,0},{5,1},{6,2},{7,3},{8,12},{9,13},{10,... | collective-permute-start | bytes 393224 | tf_op jit(solution)/shard_map/ppermute | solution.py:87
  15.6 7.6 %collective-permute-start.6 = (f32[2,16,8,128]{3,2,1,0:T(8,128)S(1)}, f32[2,16,8,128]{3,2,1,0:T(8,128)S(1)}, u32[]{:S(2)}, u32[]{:S(2)}) collective-permute-start(f32[2,16,8,128]{3,2,1,0:T(8,128)S(1)} %pad_maximum_fusion.1.refs_0_), channel_id=1, source_target_pairs={{0,6},{1,7},{2,4},{3,5},{4,2},{5,3},{6,0},{7,1},{8,14},{9,15},{10,... | collective-permute-start | bytes 393224 | tf_op jit(solution)/shard_map/ppermute | solution.py:87
  17.9 32.0 %collective-permute-start.10 = (f32[512,128]{1,0:T(8,128)S(1)}, f32[512,128]{1,0:T(8,128)S(1)}, u32[]{:S(2)}, u32[]{:S(2)}) collective-permute-start(f32[512,128]{1,0:T(8,128)S(1)} %pad_maximum_fusion.mine), channel_id=1, source_target_pairs={{0,1},{1,2},{2,3},{3,4},{4,5},{5,6},{6,7},{8,9},{9,10},{10,11},{11... | collective-permute-start | bytes 786440 | tf_op jit(solution)/shard_map/ppermute | solution.py:584
  32.1 8.7 %collective-permute-start.7 = (f32[1,5,8,128]{3,2,1,0:T(8,128)S(1)}, f32[1,5,8,128]{3,2,1,0:T(8,128)S(1)}, u32[]{:S(2)}, u32[]{:S(2)}) collective-permute-start(f32[1,5,8,128]{3,2,1,0:T(8,128)S(1)} %bitcast.45), channel_id=1, source_target_pairs={{0,8},{8,0},{16,24},{24,16},{1,9},{9,1},{17,25},{25,17},{2,10},{10... | collective-permute-start | bytes 61448 | tf_op jit(solution)/shard_map/ppermute | solution.py:87
  32.1 8.7 %collective-permute-start.8 = (f32[1,5,8,128]{3,2,1,0:T(8,128)S(1)}, f32[1,5,8,128]{3,2,1,0:T(8,128)S(1)}, u32[]{:S(2)}, u32[]{:S(2)}) collective-permute-start(f32[1,5,8,128]{3,2,1,0:T(8,128)S(1)} %bitcast.46), channel_id=1, source_target_pairs={{0,16},{8,24},{16,0},{24,8},{1,17},{9,25},{17,1},{25,9},{2,18},{10... | collective-permute-start | bytes 61448 | tf_op jit(solution)/shard_map/ppermute | solution.py:87
  34.5 6.3 %collective-permute-start.9 = (f32[1,5,8,128]{3,2,1,0:T(8,128)S(1)}, f32[1,5,8,128]{3,2,1,0:T(8,128)S(1)}, u32[]{:S(2)}, u32[]{:S(2)}) collective-permute-start(f32[1,5,8,128]{3,2,1,0:T(8,128)S(1)} %bitcast.47), channel_id=1, source_target_pairs={{0,24},{8,16},{16,8},{24,0},{1,25},{9,17},{17,9},{25,1},{2,26},{10... | collective-permute-start | bytes 61448 | tf_op jit(solution)/shard_map/ppermute | solution.py:87
  36.5 13.4 %collective-permute-start.11 = (f32[512,128]{1,0:T(8,128)S(1)}, f32[512,128]{1,0:T(8,128)S(1)}, u32[]{:S(2)}, u32[]{:S(2)}) collective-permute-start(f32[512,128]{1,0:T(8,128)S(1)} %pad_maximum_fusion.mine), channel_id=1, source_target_pairs={{1,0},{2,1},{3,2},{4,3},{5,4},{6,5},{7,6},{9,8},{10,9},{11,10},{12... | collective-permute-start | bytes 786440 | tf_op jit(solution)/shard_map/ppermute | solution.py:610
  42.0 1.4 %collective-permute-start.12 = (f32[1,32,128]{2,1,0:T(8,128)S(1)}, f32[1,32,128]{2,1,0:T(8,128)S(1)}, u32[]{:S(2)}, u32[]{:S(2)}) collective-permute-start(f32[1,32,128]{2,1,0:T(8,128)S(1)} %bitcast.54), channel_id=1, source_target_pairs={{0,1},{1,0},{2,3},{3,2},{4,5},{5,4},{6,7},{7,6},{8,9},{9,8},{10,11... | collective-permute-start | bytes 49160 | tf_op jit(solution)/shard_map/ppermute | solution.py:87
  43.4 6.0 %collective-permute-start.13 = (f32[2,32,128]{2,1,0:T(8,128)S(1)}, f32[2,32,128]{2,1,0:T(8,128)S(1)}, u32[]{:S(2)}, u32[]{:S(2)}) collective-permute-start(f32[2,32,128]{2,1,0:T(8,128)S(1)} %pad_maximum_fusion.2.refs_2_), channel_id=1, source_target_pairs={{0,2},{1,3},{2,0},{3,1},{4,6},{5,7},{6,4},{7,5},{8,10},{9,11},{10,... | collective-permute-start | bytes 98312 | tf_op jit(solution)/shard_map/ppermute | solution.py:87
  43.6 5.8 %collective-permute-start.14 = (f32[2,32,128]{2,1,0:T(8,128)S(1)}, f32[2,32,128]{2,1,0:T(8,128)S(1)}, u32[]{:S(2)}, u32[]{:S(2)}) collective-permute-start(f32[2,32,128]{2,1,0:T(8,128)S(1)} %pad_maximum_fusion.2.refs_2_), channel_id=1, source_target_pairs={{0,4},{1,5},{2,6},{3,7},{4,0},{5,1},{6,2},{7,3},{8,12},{9,13},{10,... | collective-permute-start | bytes 98312 | tf_op jit(solution)/shard_map/ppermute | solution.py:87
  45.1 4.8 %collective-permute-start.15 = (f32[2,32,128]{2,1,0:T(8,128)S(1)}, f32[2,32,128]{2,1,0:T(8,128)S(1)}, u32[]{:S(2)}, u32[]{:S(2)}) collective-permute-start(f32[2,32,128]{2,1,0:T(8,128)S(1)} %pad_maximum_fusion.2.refs_2_), channel_id=1, source_target_pairs={{0,6},{1,7},{2,4},{3,5},{4,2},{5,3},{6,0},{7,1},{8,14},{9,15},{10,... | collective-permute-start | bytes 98312 | tf_op jit(solution)/shard_map/ppermute | solution.py:87
  90.4 4.5 %collective-permute-start.16 = (f32[4,8,128]{2,1,0:T(8,128)S(1)}, f32[4,8,128]{2,1,0:T(8,128)S(1)}, u32[]{:S(2)}, u32[]{:S(2)}) collective-permute-start(f32[4,8,128]{2,1,0:T(8,128)S(1)} %get-tuple-element.26), channel_id=1, source_target_pairs={{0,8},{8,0},{16,24},{24,16},{1,9},{9,1},{17,25},{25,17},{2,10},{10... | collective-permute-start | bytes 49160 | tf_op jit(solution)/shard_map/ppermute | solution.py:663
  90.4 4.7 %collective-permute-start.17 = (f32[4,8,128]{2,1,0:T(8,128)S(1)}, f32[4,8,128]{2,1,0:T(8,128)S(1)}, u32[]{:S(2)}, u32[]{:S(2)}) collective-permute-start(f32[4,8,128]{2,1,0:T(8,128)S(1)} %get-tuple-element.25), channel_id=1, source_target_pairs={{0,16},{8,24},{16,0},{24,8},{1,17},{9,25},{17,1},{25,9},{2,18},{10... | collective-permute-start | bytes 49160 | tf_op jit(solution)/shard_map/ppermute | solution.py:663
  92.6 5.5 %collective-permute-start.18 = (f32[4,8,128]{2,1,0:T(8,128)S(1)}, f32[4,8,128]{2,1,0:T(8,128)S(1)}, u32[]{:S(2)}, u32[]{:S(2)}) collective-permute-start(f32[4,8,128]{2,1,0:T(8,128)S(1)} %get-tuple-element.24), channel_id=1, source_target_pairs={{0,24},{8,16},{16,8},{24,0},{1,25},{9,17},{17,9},{25,1},{2,26},{10... | collective-permute-start | bytes 49160 | tf_op jit(solution)/shard_map/ppermute | solution.py:663
where the time goes:
time: 100 us; the launch traced here: 99.3 us
  Pallas kernels  57.6 us (58%)
  starting transfers between devices  24.8 us (25%)
  waiting for transfers between devices  11.4 us (11%)
  other arithmetic  4.78 us (5%)
    pallas_call x7, Pallas kernels, call(): pl.pallas_call(kernel, out_shape=out_shape, in_specs=[smem()] * smems + [...  57.6 us
    ppermute x14, starting transfers between devices, gather_parts(): lax.ppermute(held, axis, [(i, i ^ have * j) for i in range(count)])  16.5 us
    ppermute x14, waiting for transfers between devices, gather_parts(): lax.ppermute(held, axis, [(i, i ^ have * j) for i in range(count)])  8.05 us
    ppermute x3, starting transfers between devices, body(): lax.ppermute(sent[k], 'orb', [(i, i ^ k) for i in range(groups)])  4.44 us
    ppermute x3, waiting for transfers between devices, body(): lax.ppermute(sent[k], 'orb', [(i, i ^ k) for i in range(groups)])  3.3 us
  transfers between devices with their start and end apart: 19, of which 8 were waited for; matrix products, arithmetic and copies ran while one was open for 5% of the time, Pallas kernels for 15%

commit v1 on v0

--- a/solution.py
+++ b/solution.py
@@ -386,7 +386,10 @@
         return found + (known < 0).astype(jnp.int32), jnp.where(lane == i, slot, lane_slot)
 
     n_levels, lane_slot = lax.fori_loop(0, orbs, rank, (jnp.int32(0), jnp.zeros((1, LANES), jnp.int32)))
-    n_batches = (n_levels + batch - 1) // batch
+    left = lax.rem(n_levels, batch)
+    short = (left > 0) & (left <= batch // 2)
+    n_whole = n_levels // batch + ((left > 0) & jnp.logical_not(short)).astype(jnp.int32)
+    n_batches = n_whole + short.astype(jnp.int32)
     first_half = lax.broadcasted_iota(jnp.int32, (1, 2 * orbs), 1) < orbs
     put_basis(cst)
 
@@ -416,7 +419,7 @@
             mom[at] = jnp.where(first_half, high, m - high).astype(jnp.bfloat16)
             return carry
 
-        lax.fori_loop(0, PLANE, prepare, 0, unroll=4)
+        lax.fori_loop(0, PLANE, prepare, 0, unroll=8)
 
     def put_plane(g, c):
         there = lax.bitwise_xor(me, g)
@@ -430,10 +433,10 @@
 
     lax.fori_loop(0, planes, put_plane, 0)
 
-    def products(g, b, first):
-        rates = [rate[b * batch + q] for q in range(batch)]
+    def products(g, b, first, width):
+        rates = [rate[b * batch + q] for q in range(width)]
         rows = []
-        for q in range(batch):
+        for q in range(width):
             tiles = [
                 (jnp.exp2(dist[g, first + h] * rates[q]) * inv[g, first + h]).astype(jnp.bfloat16) for h in range(unit)
             ]
@@ -484,21 +487,36 @@
 
                     lax.fori_loop(0, units[g], measure, 0)
 
+        nowhere = acc.shape[1] - 1
+
         def step(i, at):
             g, b, u = at
             for _ in range(steps):
-                acc[g, b] = acc[g, b] + products(g, b, unit * u)
+                acc[g, b] = acc[g, b] + products(g, b, unit * u, batch)
                 wrap = u + 1 >= units[g]
                 later = jnp.where(wrap, b + 1, b)
-                over, last = later >= n_batches, g + 1 >= share
+                over, last = later >= n_whole, g + 1 >= share
                 u = jnp.where(wrap, 0, u + 1)
-                b = jnp.where(over, jnp.where(last, n_batches, 0), later)
+                b = jnp.where(over, jnp.where(last, nowhere, 0), later)
                 g = jnp.where(over & jnp.logical_not(last), g + 1, g)
             return g, b, u
 
-        work = sum(units[g] for g in range(share)) * n_batches
+        def short_step(i, at):
+            g, u, b = at
+            for _ in range(steps):
+                at_rows = (g, b, slice(0, batch // 2 * LANES))
+                acc[at_rows] = acc[at_rows] + products(g, b, unit * u, batch // 2)
+                wrap, last = u + 1 >= units[g], g + 1 >= share
+                u = jnp.where(wrap, 0, u + 1)
+                b = jnp.where(wrap & last, nowhere, b)
+                g = jnp.where(wrap & jnp.logical_not(last), g + 1, g)
+            return g, u, b
+
+        work = sum(units[g] for g in range(share))
         zero = jnp.int32(0)
-        lax.fori_loop(0, (work + steps - 1) // steps, step, (zero, zero, zero))
+        lax.fori_loop(0, (work * n_whole + steps - 1) // steps, step, (zero, zero, zero))
+        rest = jnp.where(short, (work + steps - 1) // steps, 0)
+        lax.fori_loop(0, rest, short_step, (zero, zero, n_whole))
 
         def finish(g, x):
             def choose(b, add):

time: 100 us -> 100 us (level); the launches traced: 99.3 us -> 101 us
  Pallas kernels: 57.6 us -> 59.3 us
    pallas_call x7, Pallas kernels: 57.6 us -> 59.3 us  [call(): pl.pallas_call(kernel, out_shape=out_shape, in_specs=[smem()] * smems + [...]
where the time goes in v1:
time: 100 us; the launch traced here: 101 us
  Pallas kernels  59.3 us (59%)
  starting transfers between devices  24.7 us (25%)
  waiting for transfers between devices  11.5 us (12%)
  other arithmetic  4.78 us (5%)
    pallas_call x7, Pallas kernels, call(): pl.pallas_call(kernel, out_shape=out_shape, in_specs=[smem()] * smems + [...  59.3 us
    ppermute x14, starting transfers between devices, gather_parts(): lax.ppermute(held, axis, [(i, i ^ have * j) for i in range(count)])  16.4 us
    ppermute x14, waiting for transfers between devices, gather_parts(): lax.ppermute(held, axis, [(i, i ^ have * j) for i in range(count)])  7.95 us
    ppermute x3, starting transfers between devices, body(): lax.ppermute(sent[k], 'orb', [(i, i ^ k) for i in range(groups)])  4.44 us
    ppermute x3, waiting for transfers between devices, body(): lax.ppermute(sent[k], 'orb', [(i, i ^ k) for i in range(groups)])  3.52 us
  transfers between devices with their start and end apart: 19, of which 8 were waited for; matrix products, arithmetic and copies ran while one was open for 5% of the time, Pallas kernels for 15%

profile of v1, /device:TPU:4, one launch (start us, length us, event | category | flops | bytes accessed | tf_op | source)
XLA Modules:
  0.0 101.1 jit_solution(10193431321131568673)
XLA Ops:
  0.6 1.6 %collective-permute-start = (f32[1,8,16,128]{3,2,1,0:T(8,128)}, f32[1,8,16,128]{3,2,1,0:T(8,128)S(1)}, u32[]{:S(2)}, u32[]{:S(2)}) collective-permute-start(f32[1,8,16,128]{3,2,1,0:T(8,128)} %bitcast.56), channel_id=1, source_target_pairs={{0,8},{8,0},{16,24},{24,16},{1,9},{9,1},{17,25},{25,17},{2,10},{10... | collective-permute-start | bytes 196616 | tf_op jit(solution)/shard_map/ppermute | solution.py:87
  2.3 2.6 %collective-permute-start.1 = (f32[1,8,16,128]{3,2,1,0:T(8,128)}, f32[1,8,16,128]{3,2,1,0:T(8,128)S(1)}, u32[]{:S(2)}, u32[]{:S(2)}) collective-permute-start(f32[1,8,16,128]{3,2,1,0:T(8,128)} %bitcast.57), channel_id=1, source_target_pairs={{0,16},{8,24},{16,0},{24,8},{1,17},{9,25},{17,1},{25,9},{2,18},{10... | collective-permute-start | bytes 196616 | tf_op jit(solution)/shard_map/ppermute | solution.py:87
  4.9 0.2 collective-permute-start.2
  5.1 0.7 multiply_bitcast_fusion
  5.8 0.7 convert_element_type.8
  6.4 0.7 broadcast_multiply_fusion.rates_of
  7.1 0.1 pad.20.clone
  7.2 1.0 maximum_maximum_fusion
  8.1 0.1 pad_add_fusion.1.meta
  8.2 0.0 collective-permute-done
  8.2 1.6 %collective-permute-done.1 = f32[1,8,16,128]{3,2,1,0:T(8,128)S(1)} collective-permute-done((f32[1,8,16,128]{3,2,1,0:T(8,128)}, f32[1,8,16,128]{3,2,1,0:T(8,128)S(1)}, u32[]{:S(2)}, u32[]{:S(2)}) %collective-permute-start.1) | collective-permute-done | bytes 65568 | tf_op jit(solution)/shard_map/ppermute | solution.py:87
  9.8 1.4 %collective-permute-done.2 = f32[1,8,16,128]{3,2,1,0:T(8,128)S(1)} collective-permute-done((f32[1,8,16,128]{3,2,1,0:T(8,128)}, f32[1,8,16,128]{3,2,1,0:T(8,128)S(1)}, u32[]{:S(2)}, u32[]{:S(2)}) %collective-permute-start.2) | collective-permute-done | bytes 65568 | tf_op jit(solution)/shard_map/ppermute | solution.py:87
  11.2 1.1 %charge.1 = f32[16,8,128]{2,1,0:T(8,128)S(1)} custom-call(s32[2]{0:T(128)S(1)} %pad_add_fusion.1.meta, f32[8,16,128]{2,1,0:T(8,128)S(1)} %get-tuple-element.28.own, f32[16,128]{1,0:T(8,128)S(1)} %get-tuple-element.29.partial, f32[8,16,128]{2,1,0:T(8,128)S(1)} %bitcast.39, f32[8,16,128]{2,1,0:T(8,128)S(1)} %bitcast.41, f32[8,16,128]{2,1,0:T(8,128)S(1)} %bitcast.43), custom_call_target="tpu_custom_call" | custom-call | tf_op jit(solution)/shard_map/charge/pallas_call | solution.py:559
  12.3 0.0 collective-permute-start.3
  12.3 0.9 pad_maximum_fusion.mine
  13.1 0.4 collective-permute-done.3
  13.5 1.6 %collective-permute-start.4 = (f32[2,16,8,128]{3,2,1,0:T(8,128)S(1)}, f32[2,16,8,128]{3,2,1,0:T(8,128)S(1)}, u32[]{:S(2)}, u32[]{:S(2)}) collective-permute-start(f32[2,16,8,128]{3,2,1,0:T(8,128)S(1)} %pad_maximum_fusion.1.refs_0_), channel_id=1, source_target_pairs={{0,2},{1,3},{2,0},{3,1},{4,6},{5,7},{6,4},{7,5},{8,10},{9,11},{10,... | collective-permute-start | bytes 393224 | tf_op jit(solution)/shard_map/ppermute | solution.py:87
  15.1 0.5 collective-permute-start.5
  15.6 1.5 %collective-permute-start.6 = (f32[2,16,8,128]{3,2,1,0:T(8,128)S(1)}, f32[2,16,8,128]{3,2,1,0:T(8,128)S(1)}, u32[]{:S(2)}, u32[]{:S(2)}) collective-permute-start(f32[2,16,8,128]{3,2,1,0:T(8,128)S(1)} %pad_maximum_fusion.1.refs_0_), channel_id=1, source_target_pairs={{0,6},{1,7},{2,4},{3,5},{4,2},{5,3},{6,0},{7,1},{8,14},{9,15},{10,... | collective-permute-start | bytes 393224 | tf_op jit(solution)/shard_map/ppermute | solution.py:87
  17.1 0.8 pad_add_fusion.lists
  17.9 1.9 %collective-permute-start.10 = (f32[512,128]{1,0:T(8,128)S(1)}, f32[512,128]{1,0:T(8,128)S(1)}, u32[]{:S(2)}, u32[]{:S(2)}) collective-permute-start(f32[512,128]{1,0:T(8,128)S(1)} %pad_maximum_fusion.mine), channel_id=1, source_target_pairs={{0,1},{1,2},{2,3},{3,4},{4,5},{5,6},{6,7},{8,9},{9,10},{10,11},{11... | collective-permute-start | bytes 786440 | tf_op jit(solution)/shard_map/ppermute | solution.py:602
  19.8 0.0 collective-permute-done.4.refs_1_
  19.8 3.4 %collective-permute-done.5.refs_2_ = f32[2,16,8,128]{3,2,1,0:T(8,128)S(1)} collective-permute-done((f32[2,16,8,128]{3,2,1,0:T(8,128)S(1)}, f32[2,16,8,128]{3,2,1,0:T(8,128)S(1)}, u32[]{:S(2)}, u32[]{:S(2)}) %collective-permute-start.5) | collective-permute-done | bytes 131104 | tf_op jit(solution)/shard_map/ppermute | solution.py:87
  23.2 0.0 collective-permute-done.6.refs_3_
  23.2 9.0 %hartree.1 = (f32[5,8,128]{2,1,0:T(8,128)S(1)}, f32[48,8,128]{2,1,0:T(8,128)S(1)}, f32[4,44,8,128]{3,2,1,0:T(8,128)S(1)}) custom-call(s32[2]{0:T(128)S(1)} %pad_add_fusion.1.meta, s32[16,69]{1,0:T(8,128)S(1)} %pad_add_fusion.lists, f32[1,128]{1,0:T(1,128)S(1)} %pad_bitcast_fusion.marks, f32[512,128]{1,0:T(8,128)S(1)} %pad_maximum_fusion.mine, ...), custom_call_target="tpu_custom_call" | custom-call | tf_op jit(solution)/shard_map/hartree/pallas_call | solution.py:559
  32.2 0.0 collective-permute-start.7
  32.2 2.4 %collective-permute-start.8 = (f32[1,5,8,128]{3,2,1,0:T(8,128)S(1)}, f32[1,5,8,128]{3,2,1,0:T(8,128)S(1)}, u32[]{:S(2)}, u32[]{:S(2)}) collective-permute-start(f32[1,5,8,128]{3,2,1,0:T(8,128)S(1)} %bitcast.46), channel_id=1, source_target_pairs={{0,16},{8,24},{16,0},{24,8},{1,17},{9,25},{17,1},{25,9},{2,18},{10... | collective-permute-start | bytes 61448 | tf_op jit(solution)/shard_map/ppermute | solution.py:87
  34.6 2.0 %collective-permute-start.9 = (f32[1,5,8,128]{3,2,1,0:T(8,128)S(1)}, f32[1,5,8,128]{3,2,1,0:T(8,128)S(1)}, u32[]{:S(2)}, u32[]{:S(2)}) collective-permute-start(f32[1,5,8,128]{3,2,1,0:T(8,128)S(1)} %bitcast.47), channel_id=1, source_target_pairs={{0,24},{8,16},{16,8},{24,0},{1,25},{9,17},{17,9},{25,1},{2,26},{10... | collective-permute-start | bytes 61448 | tf_op jit(solution)/shard_map/ppermute | solution.py:87
  36.6 1.9 %collective-permute-start.11 = (f32[512,128]{1,0:T(8,128)S(1)}, f32[512,128]{1,0:T(8,128)S(1)}, u32[]{:S(2)}, u32[]{:S(2)}) collective-permute-start(f32[512,128]{1,0:T(8,128)S(1)} %pad_maximum_fusion.mine), channel_id=1, source_target_pairs={{1,0},{2,1},{3,2},{4,3},{5,4},{6,5},{7,6},{9,8},{10,9},{11,10},{12... | collective-permute-start | bytes 786440 | tf_op jit(solution)/shard_map/ppermute | solution.py:628
  38.6 2.4 %pairs.2.refs_0_ = f32[2,44,128,128]{3,2,1,0:T(8,128)S(1)} custom-call(s32[2]{0:T(128)S(1)} %pad_add_fusion.1.meta, s32[16,69]{1,0:T(8,128)S(1)} %pad_add_fusion.lists, f32[48,8,128]{2,1,0:T(8,128)S(1)} %get-tuple-element.17.pts, f32[4,44,8,128]{3,2,1,0:T(8,128)S(1)} %get-tuple-element.21.src), custom_call_target="tpu_custom_call" | custom-call | tf_op jit(solution)/shard_map/pairs/pallas_call | solution.py:559
  41.0 0.0 collective-permute-done.9
  41.0 0.0 collective-permute-done.8
  41.0 0.0 collective-permute-done.7
  41.0 1.2 %combine.1 = (f32[16,128]{1,0:T(8,128)}, f32[32,128]{1,0:T(8,128)S(1)}) custom-call(s32[2]{0:T(128)S(1)} %pad_add_fusion.1.meta, f32[5,8,128]{2,1,0:T(8,128)S(1)} %get-tuple-element.16.refs_0_, f32[5,8,128]{2,1,0:T(8,128)S(1)} %bitcast.48, f32[5,8,128]{2,1,0:T(8,128)S(1)} %bitcast.51, f32[5,8,128]{2,1,0:T(8,128)S(1)} %bitcast.53), custom_call_target="tpu_custom_call" | custom-call | tf_op jit(solution)/shard_map/combine/pallas_call | solution.py:559
  42.2 0.5 collective-permute-start.12
  42.7 0.8 collective-permute-done.12
  43.5 0.3 collective-permute-start.13
  43.8 1.3 %collective-permute-start.14 = (f32[2,32,128]{2,1,0:T(8,128)S(1)}, f32[2,32,128]{2,1,0:T(8,128)S(1)}, u32[]{:S(2)}, u32[]{:S(2)}) collective-permute-start(f32[2,32,128]{2,1,0:T(8,128)S(1)} %pad_maximum_fusion.2.refs_2_), channel_id=1, source_target_pairs={{0,4},{1,5},{2,6},{3,7},{4,0},{5,1},{6,2},{7,3},{8,12},{9,13},{10,... | collective-permute-start | bytes 98312 | tf_op jit(solution)/shard_map/ppermute | solution.py:87
  45.1 1.9 %collective-permute-start.15 = (f32[2,32,128]{2,1,0:T(8,128)S(1)}, f32[2,32,128]{2,1,0:T(8,128)S(1)}, u32[]{:S(2)}, u32[]{:S(2)}) collective-permute-start(f32[2,32,128]{2,1,0:T(8,128)S(1)} %pad_maximum_fusion.2.refs_2_), channel_id=1, source_target_pairs={{0,6},{1,7},{2,4},{3,5},{4,2},{5,3},{6,0},{7,1},{8,14},{9,15},{10,... | collective-permute-start | bytes 98312 | tf_op jit(solution)/shard_map/ppermute | solution.py:87
  47.0 0.1 maximum_convert_fusion.levels
  47.1 2.4 %pairs.3.refs_1_ = f32[2,44,128,128]{3,2,1,0:T(8,128)S(1)} custom-call(s32[2]{0:T(128)S(1)} %pad_add_fusion.1.meta, s32[16,69]{1,0:T(8,128)S(1)} %pad_add_fusion.lists, f32[48,8,128]{2,1,0:T(8,128)S(1)} %get-tuple-element.17.pts, f32[4,44,8,128]{3,2,1,0:T(8,128)S(1)} %get-tuple-element.21.src), custom_call_target="tpu_custom_call" | custom-call | tf_op jit(solution)/shard_map/pairs/pallas_call | solution.py:559
  49.5 0.0 collective-permute-done.13.refs_3_
  49.5 0.0 collective-permute-done.14.refs_4_
  49.6 0.4 collective-permute-done.15.refs_5_
  49.9 0.0 collective-permute-done.10.before
  49.9 0.0 collective-permute-done.11.after
  49.9 42.0 %orbitals.1 = f32[4,4,8,128]{3,2,1,0:T(8,128)S(1)} custom-call(s32[2]{0:T(128)S(1)} %pad_add_fusion.1.meta, s32[16,69]{1,0:T(8,128)S(1)} %pad_add_fusion.lists, s32[32]{0:T(128)S(1)} %maximum_convert_fusion.levels, f32[32]{0:T(128)S(1)} %broadcast_multiply_fusion.rates_of, f32[48,8,128]{2,1,0:T(8,128)S(1)} %get-tuple-element.17.pts, ...), custom_call_target="tpu_custom_call" | custom-call | tf_op jit(solution)/shard_map/orbitals/pallas_call | solution.py:559
  91.9 0.1 collective-permute-start.16
  92.0 2.4 %collective-permute-start.17 = (f32[4,8,128]{2,1,0:T(8,128)S(1)}, f32[4,8,128]{2,1,0:T(8,128)S(1)}, u32[]{:S(2)}, u32[]{:S(2)}) collective-permute-start(f32[4,8,128]{2,1,0:T(8,128)S(1)} %get-tuple-element.25), channel_id=1, source_target_pairs={{0,16},{8,24},{16,0},{24,8},{1,17},{9,25},{17,1},{25,9},{2,18},{10... | collective-permute-start | bytes 49160 | tf_op jit(solution)/shard_map/ppermute | solution.py:681
  94.4 2.0 %collective-permute-start.18 = (f32[4,8,128]{2,1,0:T(8,128)S(1)}, f32[4,8,128]{2,1,0:T(8,128)S(1)}, u32[]{:S(2)}, u32[]{:S(2)}) collective-permute-start(f32[4,8,128]{2,1,0:T(8,128)S(1)} %get-tuple-element.24), channel_id=1, source_target_pairs={{0,24},{8,16},{16,8},{24,0},{1,25},{9,17},{17,9},{25,1},{2,26},{10... | collective-permute-start | bytes 49160 | tf_op jit(solution)/shard_map/ppermute | solution.py:681
  96.4 0.0 collective-permute-done.16.refs_1_
  96.4 0.3 collective-permute-done.17.refs_2_
  96.7 3.2 %collective-permute-done.18.refs_3_ = f32[4,8,128]{2,1,0:T(8,128)S(1)} collective-permute-done((f32[4,8,128]{2,1,0:T(8,128)S(1)}, f32[4,8,128]{2,1,0:T(8,128)S(1)}, u32[]{:S(2)}, u32[]{:S(2)}) %collective-permute-start.18) | collective-permute-done | bytes 16416 | tf_op jit(solution)/shard_map/ppermute | solution.py:681
  99.9 1.2 %place.1 = f32[8,16,128]{2,1,0:T(8,128)} custom-call(s32[2]{0:T(128)S(1)} %pad_add_fusion.1.meta, f32[4,8,128]{2,1,0:T(8,128)S(1)} %get-tuple-element.27.refs_0_, f32[4,8,128]{2,1,0:T(8,128)S(1)} %collective-permute-done.16.refs_1_, f32[4,8,128]{2,1,0:T(8,128)S(1)} %collective-permute-done.17.refs_2_, f32[4,8,128]{2,1,0:T(8,128)S(1)} %collective-permute-done.18.refs_3_), custom_call_target="tpu_custom_call" | custom-call | tf_op jit(solution)/shard_map/place/pallas_call | solution.py:559
  (9 shorter events, 0.0 us)
Async XLA Ops:
  0.6 7.6 %collective-permute-start = (f32[1,8,16,128]{3,2,1,0:T(8,128)}, f32[1,8,16,128]{3,2,1,0:T(8,128)S(1)}, u32[]{:S(2)}, u32[]{:S(2)}) collective-permute-start(f32[1,8,16,128]{3,2,1,0:T(8,128)} %bitcast.56), channel_id=1, source_target_pairs={{0,8},{8,0},{16,24},{24,16},{1,9},{9,1},{17,25},{25,17},{2,10},{10... | collective-permute-start | bytes 196616 | tf_op jit(solution)/shard_map/ppermute | solution.py:87
  2.3 7.5 %collective-permute-start.1 = (f32[1,8,16,128]{3,2,1,0:T(8,128)}, f32[1,8,16,128]{3,2,1,0:T(8,128)S(1)}, u32[]{:S(2)}, u32[]{:S(2)}) collective-permute-start(f32[1,8,16,128]{3,2,1,0:T(8,128)} %bitcast.57), channel_id=1, source_target_pairs={{0,16},{8,24},{16,0},{24,8},{1,17},{9,25},{17,1},{25,9},{2,18},{10... | collective-permute-start | bytes 196616 | tf_op jit(solution)/shard_map/ppermute | solution.py:87
  4.9 6.3 %collective-permute-start.2 = (f32[1,8,16,128]{3,2,1,0:T(8,128)}, f32[1,8,16,128]{3,2,1,0:T(8,128)S(1)}, u32[]{:S(2)}, u32[]{:S(2)}) collective-permute-start(f32[1,8,16,128]{3,2,1,0:T(8,128)} %bitcast.58), channel_id=1, source_target_pairs={{0,24},{8,16},{16,8},{24,0},{1,25},{9,17},{17,9},{25,1},{2,26},{10... | collective-permute-start | bytes 196616 | tf_op jit(solution)/shard_map/ppermute | solution.py:87
  12.3 1.3 %collective-permute-start.3 = (f32[1,16,8,128]{3,2,1,0:T(8,128)S(1)}, f32[1,16,8,128]{3,2,1,0:T(8,128)S(1)}, u32[]{:S(2)}, u32[]{:S(2)}) collective-permute-start(f32[1,16,8,128]{3,2,1,0:T(8,128)S(1)} %bitcast.37), channel_id=1, source_target_pairs={{0,1},{1,0},{2,3},{3,2},{4,5},{5,4},{6,7},{7,6},{8,9},{9,8},{10,11... | collective-permute-start | bytes 196616 | tf_op jit(solution)/shard_map/ppermute | solution.py:87
  13.5 6.3 %collective-permute-start.4 = (f32[2,16,8,128]{3,2,1,0:T(8,128)S(1)}, f32[2,16,8,128]{3,2,1,0:T(8,128)S(1)}, u32[]{:S(2)}, u32[]{:S(2)}) collective-permute-start(f32[2,16,8,128]{3,2,1,0:T(8,128)S(1)} %pad_maximum_fusion.1.refs_0_), channel_id=1, source_target_pairs={{0,2},{1,3},{2,0},{3,1},{4,6},{5,7},{6,4},{7,5},{8,10},{9,11},{10,... | collective-permute-start | bytes 393224 | tf_op jit(solution)/shard_map/ppermute | solution.py:87
  15.1 8.1 %collective-permute-start.5 = (f32[2,16,8,128]{3,2,1,0:T(8,128)S(1)}, f32[2,16,8,128]{3,2,1,0:T(8,128)S(1)}, u32[]{:S(2)}, u32[]{:S(2)}) collective-permute-start(f32[2,16,8,128]{3,2,1,0:T(8,128)S(1)} %pad_maximum_fusion.1.refs_0_), channel_id=1, source_target_pairs={{0,4},{1,5},{2,6},{3,7},{4,0},{5,1},{6,2},{7,3},{8,12},{9,13},{10,... | collective-permute-start | bytes 393224 | tf_op jit(solution)/shard_map/ppermute | solution.py:87
  15.6 7.6 %collective-permute-start.6 = (f32[2,16,8,128]{3,2,1,0:T(8,128)S(1)}, f32[2,16,8,128]{3,2,1,0:T(8,128)S(1)}, u32[]{:S(2)}, u32[]{:S(2)}) collective-permute-start(f32[2,16,8,128]{3,2,1,0:T(8,128)S(1)} %pad_maximum_fusion.1.refs_0_), channel_id=1, source_target_pairs={{0,6},{1,7},{2,4},{3,5},{4,2},{5,3},{6,0},{7,1},{8,14},{9,15},{10,... | collective-permute-start | bytes 393224 | tf_op jit(solution)/shard_map/ppermute | solution.py:87
  17.9 32.1 %collective-permute-start.10 = (f32[512,128]{1,0:T(8,128)S(1)}, f32[512,128]{1,0:T(8,128)S(1)}, u32[]{:S(2)}, u32[]{:S(2)}) collective-permute-start(f32[512,128]{1,0:T(8,128)S(1)} %pad_maximum_fusion.mine), channel_id=1, source_target_pairs={{0,1},{1,2},{2,3},{3,4},{4,5},{5,6},{6,7},{8,9},{9,10},{10,11},{11... | collective-permute-start | bytes 786440 | tf_op jit(solution)/shard_map/ppermute | solution.py:602
  32.2 8.8 %collective-permute-start.7 = (f32[1,5,8,128]{3,2,1,0:T(8,128)S(1)}, f32[1,5,8,128]{3,2,1,0:T(8,128)S(1)}, u32[]{:S(2)}, u32[]{:S(2)}) collective-permute-start(f32[1,5,8,128]{3,2,1,0:T(8,128)S(1)} %bitcast.45), channel_id=1, source_target_pairs={{0,8},{8,0},{16,24},{24,16},{1,9},{9,1},{17,25},{25,17},{2,10},{10... | collective-permute-start | bytes 61448 | tf_op jit(solution)/shard_map/ppermute | solution.py:87
  32.2 8.8 %collective-permute-start.8 = (f32[1,5,8,128]{3,2,1,0:T(8,128)S(1)}, f32[1,5,8,128]{3,2,1,0:T(8,128)S(1)}, u32[]{:S(2)}, u32[]{:S(2)}) collective-permute-start(f32[1,5,8,128]{3,2,1,0:T(8,128)S(1)} %bitcast.46), channel_id=1, source_target_pairs={{0,16},{8,24},{16,0},{24,8},{1,17},{9,25},{17,1},{25,9},{2,18},{10... | collective-permute-start | bytes 61448 | tf_op jit(solution)/shard_map/ppermute | solution.py:87
  34.6 6.4 %collective-permute-start.9 = (f32[1,5,8,128]{3,2,1,0:T(8,128)S(1)}, f32[1,5,8,128]{3,2,1,0:T(8,128)S(1)}, u32[]{:S(2)}, u32[]{:S(2)}) collective-permute-start(f32[1,5,8,128]{3,2,1,0:T(8,128)S(1)} %bitcast.47), channel_id=1, source_target_pairs={{0,24},{8,16},{16,8},{24,0},{1,25},{9,17},{17,9},{25,1},{2,26},{10... | collective-permute-start | bytes 61448 | tf_op jit(solution)/shard_map/ppermute | solution.py:87
  36.6 13.3 %collective-permute-start.11 = (f32[512,128]{1,0:T(8,128)S(1)}, f32[512,128]{1,0:T(8,128)S(1)}, u32[]{:S(2)}, u32[]{:S(2)}) collective-permute-start(f32[512,128]{1,0:T(8,128)S(1)} %pad_maximum_fusion.mine), channel_id=1, source_target_pairs={{1,0},{2,1},{3,2},{4,3},{5,4},{6,5},{7,6},{9,8},{10,9},{11,10},{12... | collective-permute-start | bytes 786440 | tf_op jit(solution)/shard_map/ppermute | solution.py:628
  42.2 1.3 %collective-permute-start.12 = (f32[1,32,128]{2,1,0:T(8,128)S(1)}, f32[1,32,128]{2,1,0:T(8,128)S(1)}, u32[]{:S(2)}, u32[]{:S(2)}) collective-permute-start(f32[1,32,128]{2,1,0:T(8,128)S(1)} %bitcast.54), channel_id=1, source_target_pairs={{0,1},{1,0},{2,3},{3,2},{4,5},{5,4},{6,7},{7,6},{8,9},{9,8},{10,11... | collective-permute-start | bytes 49160 | tf_op jit(solution)/shard_map/ppermute | solution.py:87
  43.5 6.0 %collective-permute-start.13 = (f32[2,32,128]{2,1,0:T(8,128)S(1)}, f32[2,32,128]{2,1,0:T(8,128)S(1)}, u32[]{:S(2)}, u32[]{:S(2)}) collective-permute-start(f32[2,32,128]{2,1,0:T(8,128)S(1)} %pad_maximum_fusion.2.refs_2_), channel_id=1, source_target_pairs={{0,2},{1,3},{2,0},{3,1},{4,6},{5,7},{6,4},{7,5},{8,10},{9,11},{10,... | collective-permute-start | bytes 98312 | tf_op jit(solution)/shard_map/ppermute | solution.py:87
  43.8 5.8 %collective-permute-start.14 = (f32[2,32,128]{2,1,0:T(8,128)S(1)}, f32[2,32,128]{2,1,0:T(8,128)S(1)}, u32[]{:S(2)}, u32[]{:S(2)}) collective-permute-start(f32[2,32,128]{2,1,0:T(8,128)S(1)} %pad_maximum_fusion.2.refs_2_), channel_id=1, source_target_pairs={{0,4},{1,5},{2,6},{3,7},{4,0},{5,1},{6,2},{7,3},{8,12},{9,13},{10,... | collective-permute-start | bytes 98312 | tf_op jit(solution)/shard_map/ppermute | solution.py:87
  45.1 4.8 %collective-permute-start.15 = (f32[2,32,128]{2,1,0:T(8,128)S(1)}, f32[2,32,128]{2,1,0:T(8,128)S(1)}, u32[]{:S(2)}, u32[]{:S(2)}) collective-permute-start(f32[2,32,128]{2,1,0:T(8,128)S(1)} %pad_maximum_fusion.2.refs_2_), channel_id=1, source_target_pairs={{0,6},{1,7},{2,4},{3,5},{4,2},{5,3},{6,0},{7,1},{8,14},{9,15},{10,... | collective-permute-start | bytes 98312 | tf_op jit(solution)/shard_map/ppermute | solution.py:87
  91.9 4.5 %collective-permute-start.16 = (f32[4,8,128]{2,1,0:T(8,128)S(1)}, f32[4,8,128]{2,1,0:T(8,128)S(1)}, u32[]{:S(2)}, u32[]{:S(2)}) collective-permute-start(f32[4,8,128]{2,1,0:T(8,128)S(1)} %get-tuple-element.26), channel_id=1, source_target_pairs={{0,8},{8,0},{16,24},{24,16},{1,9},{9,1},{17,25},{25,17},{2,10},{10... | collective-permute-start | bytes 49160 | tf_op jit(solution)/shard_map/ppermute | solution.py:681
  92.0 4.7 %collective-permute-start.17 = (f32[4,8,128]{2,1,0:T(8,128)S(1)}, f32[4,8,128]{2,1,0:T(8,128)S(1)}, u32[]{:S(2)}, u32[]{:S(2)}) collective-permute-start(f32[4,8,128]{2,1,0:T(8,128)S(1)} %get-tuple-element.25), channel_id=1, source_target_pairs={{0,16},{8,24},{16,0},{24,8},{1,17},{9,25},{17,1},{25,9},{2,18},{10... | collective-permute-start | bytes 49160 | tf_op jit(solution)/shard_map/ppermute | solution.py:681
  94.4 5.5 %collective-permute-start.18 = (f32[4,8,128]{2,1,0:T(8,128)S(1)}, f32[4,8,128]{2,1,0:T(8,128)S(1)}, u32[]{:S(2)}, u32[]{:S(2)}) collective-permute-start(f32[4,8,128]{2,1,0:T(8,128)S(1)} %get-tuple-element.24), channel_id=1, source_target_pairs={{0,24},{8,16},{16,8},{24,0},{1,25},{9,17},{17,9},{25,1},{2,26},{10... | collective-permute-start | bytes 49160 | tf_op jit(solution)/shard_map/ppermute | solution.py:681
